TPU v7x, 512 devices: a whole 4x4x16 slice. The times are simulated.
512 devices in a mesh: space: 32 (over z, core), tm: 16 (over x, y).
Axes of the slice: x: 4, y: 4, z: 16, core: 2. Of those that a mesh axis runs over, the one named last changes fastest.
Arguments:
- recordings: bfloat16 [2, 3, 512, 32768], P(None, None, 'space', 'tm'), may hold values from -30 to 30
- owner: int32 [512, 1], P('space'), may hold values from 0 to 31; in each aligned block of 16 rows (0 to 15, 16 to 31, ...) at most 2 rows name the same one
- valid_range: int32 [512, 2], P('space'), may hold values from 0 to 32768, as said below
- bin_mask: int32 [512, 96], P('space'), may hold values 0 or 1
Outputs:
- adjoint: bfloat16 [3, 2048, 32768], P(None, 'space', 'tm')
Inputs may be any that keep to these rules, and one draw needn't show every extreme that they name: `owner`: among the 16 receivers listed on one index of space, no subdomain owns more than 2; some subdomain owns exactly 2 of them. `valid_range`: column 0 is below column 1 in every row.
All inputs are finite; a program needn't handle non-finite values. No bound on the sum of `bin_mask` on one device may be relied on, other than what follows from the above.
Results may differ from a plain program's by a relative error of at most 0.013.
Values may be sent and summed in bfloat16 or wider, within the bound.
A program may use at most 128 MiB of HBM per device.

v0:
```python
import math
import jax
import jax.numpy as jnp
from jax import lax
from jax.sharding import PartitionSpec as P

BINS = 96
HOP = 256
HALO = 1024
KERNEL = 2304
WATER = 0.1
EPSILON = 1e-06


def with_halo(block, sides, width):
    for axis, dim in sides:
        count = lax.axis_size(axis)
        forward = [(i, i + 1) for i in range(count - 1)]
        backward = [(target, source) for source, target in forward]
        low = lax.ppermute(
            lax.slice_in_dim(block, block.shape[dim] - width, None, axis=dim), axis, forward
        )
        high = lax.ppermute(lax.slice_in_dim(block, 0, width, axis=dim), axis, backward)
        block = jnp.concatenate([low, block, high], axis=dim)
    return block


def shifted(block, axis, distance):
    devices = range(lax.axis_size(axis))
    route = [(i - distance, i) for i in devices if i - distance in devices]
    return lax.ppermute(block, axis, route)


def cq_kernel(kern_len, bins):
    octave_bins = bins // 8
    index = jnp.arange(bins).astype(jnp.float32)
    freq = 0.25 * jnp.exp2((index - (bins - 1)) / octave_bins)
    quality = 1.0 / (2.0 ** (1.0 / octave_bins) - 1.0)
    support = jnp.minimum(quality / freq, float(kern_len))
    offset = jnp.arange(kern_len).astype(jnp.float32) - 0.5 * (kern_len - 1)
    ratio = offset[:, None] / support[None, :]
    window = jnp.where(jnp.abs(ratio) < 0.5, 0.5 + 0.5 * jnp.cos(2.0 * math.pi * ratio), 0.0)
    window = window / jnp.sqrt(jnp.sum(window * window, axis=0, keepdims=True))
    cycles = offset[:, None] * freq[None, :]
    phase = cycles - jnp.floor(cycles)
    table = jnp.concatenate(
        [window * jnp.cos(2.0 * math.pi * phase), -window * jnp.sin(2.0 * math.pi * phase)], axis=1
    )
    return table.astype(jnp.bfloat16)


def adjoint_of(syn_re, syn_im, obs_re, obs_im, weight):
    level = (
        WATER * jnp.mean(obs_re * obs_re + obs_im * obs_im, axis=(-2, -1), keepdims=True) + EPSILON
    )
    syn_norm = jnp.sqrt(syn_re * syn_re + syn_im * syn_im + level)
    obs_norm = jnp.sqrt(obs_re * obs_re + obs_im * obs_im + level)
    diff_re = weight * (syn_re / syn_norm - obs_re / obs_norm)
    diff_im = weight * (syn_im / syn_norm - obs_im / obs_norm)
    inner = (syn_re * diff_re + syn_im * diff_im) / (syn_norm * syn_norm * syn_norm)
    return (diff_re / syn_norm - syn_re * inner, diff_im / syn_norm - syn_im * inner)


def analyse(blocks, table, frames):
    taps = table.shape[0] // HOP
    unfolded = jnp.concatenate([blocks[..., tap : tap + frames, :] for tap in range(taps)], axis=-1)
    return jnp.einsum("...fh,hk->...fk", unfolded, table, preferred_element_type=jnp.float32)


def synthesise(coefs, table, frames):
    taps = table.shape[0] // HOP
    term = jnp.einsum("...fk,hk->...fh", coefs, table, preferred_element_type=jnp.float32)
    term = term.reshape(term.shape[:-1] + (taps, HOP))
    lead = len(term.shape) - 3
    ext = jnp.zeros(coefs.shape[:-2] + (frames + taps - 1, HOP), jnp.float32)
    for tap in range(taps):
        widths = [(0, 0)] * lead + [(tap, taps - 1 - tap), (0, 0)]
        ext = ext + jnp.pad(term[..., tap, :], widths)
    return ext


def frame_weight(ranges, masks, frames_all):
    centers = jnp.arange(frames_all, dtype=jnp.int32) * HOP + HOP // 2
    inside = (ranges[:, 0:1] <= centers[None, :]) & (centers[None, :] < ranges[:, 1:2])
    return inside.astype(jnp.float32)[:, :, None] * masks.astype(jnp.float32)[:, None, :]


def misfit(coefs, weight):
    adj_re, adj_im = adjoint_of(
        coefs[0, ..., :BINS],
        coefs[0, ..., BINS:],
        coefs[1, ..., :BINS],
        coefs[1, ..., BINS:],
        weight,
    )
    joined = jnp.concatenate([adj_re, adj_im], axis=-1)
    return joined.reshape(joined.shape[:2] + (joined.shape[2] * joined.shape[3],)).astype(
        jnp.bfloat16
    )


def on_device(recordings, owner, valid_range, bin_mask):
    table = cq_kernel(KERNEL, BINS)
    margin = HALO // HOP
    width = 2 * BINS
    groups = lax.axis_size("tm")
    comps = recordings.shape[1]
    rec_dev = recordings.shape[2]
    samples_dev = recordings.shape[3]
    frames_dev = samples_dev // HOP
    rec_group = rec_dev // groups
    first_row = lax.axis_index("tm") * rec_group
    ranges = lax.dynamic_slice_in_dim(valid_range, first_row, rec_group, 0)
    masks = lax.dynamic_slice_in_dim(bin_mask, first_row, rec_group, 0)
    extended = with_halo(recordings, (("tm", 3),), HALO)
    blocks = extended.reshape(2, comps, rec_dev, frames_dev + 2 * margin, HOP)
    coefs = analyse(blocks, table, frames_dev)
    packed = coefs.astype(jnp.bfloat16).reshape(2, comps, rec_dev, frames_dev * width)
    weight = frame_weight(ranges, masks, frames_dev * groups)
    pieces = lax.all_to_all(packed, "tm", split_axis=2, concat_axis=3, tiled=True)
    items = pieces.shape[1]
    frames_all = pieces.shape[3] // width
    local_coefs = pieces.astype(jnp.float32).reshape(2, items, rec_group, frames_all, width)
    adjoint_local = misfit(local_coefs, weight)
    adjoint_back = lax.all_to_all(adjoint_local, "tm", split_axis=2, concat_axis=1, tiled=True)
    adjoint_frames = adjoint_back.reshape(comps, rec_dev, frames_dev, width)
    ext = synthesise(adjoint_frames, table, frames_dev)
    flat = ext.reshape(comps, rec_dev, (frames_dev + 2 * margin) * HOP)
    middle = flat[:, :, HALO : HALO + samples_dev]
    from_before = shifted(flat[:, :, HALO + samples_dev :].astype(jnp.bfloat16), "tm", 1).astype(
        jnp.float32
    )
    from_after = shifted(flat[:, :, :HALO].astype(jnp.bfloat16), "tm", -1).astype(jnp.float32)
    middle = middle.at[:, :, :HALO].add(from_before)
    middle = middle.at[:, :, samples_dev - HALO :].add(from_after)
    series = middle.astype(jnp.bfloat16)
    count = lax.axis_size("space")
    most = max(2, 3 * rec_dev // (2 * count))
    target = owner[:, 0]
    onehot = (target[:, None] == jnp.arange(count, dtype=jnp.int32)[None, :]).astype(jnp.int32)
    before = jnp.cumsum(onehot, axis=0) - onehot
    rank = jnp.sum(before * onehot, axis=1)
    slot = target * most + rank
    select = (jnp.arange(count * most, dtype=jnp.int32)[:, None] == slot[None, :]).astype(
        jnp.bfloat16
    )
    outgoing = jnp.einsum("sr,crt->cst", select, series, preferred_element_type=jnp.float32).astype(
        jnp.bfloat16
    )
    return lax.all_to_all(outgoing, "space", split_axis=1, concat_axis=1, tiled=True)


def solution(mesh):
    return jax.shard_map(
        on_device,
        mesh=mesh,
        in_specs=(
            P(None, None, "space", "tm"),
            P("space", None),
            P("space", None),
            P("space", None),
        ),
        out_specs=P(None, "space", "tm"),
        check_vma=False,
    )
```

profile of v0, /device:TPU:25, one launch (start us, length us, event | category | flops | bytes accessed | tf_op | source)
XLA Modules:
  0.0 347.0 jit_solution(11848009665123763137)
XLA Ops:
  0.0 1.1 fusion.24
  1.1 2.8 collective-permute-start
  3.9 2.5 collective-permute-start.1
  6.5 3.4 multiply_reduce_fusion
  9.9 6.7 %multiply_convert_fusion.3 = (bf16[2304,96]{0,1:T(8,128)(2,1)S(1)}, bf16[2304,96]{0,1:T(8,128)(2,1)S(1)}) fusion(f32[96]{0:T(128)S(1)} %get-tuple-element.51, f32[2304]{0:T(1024)S(1)} %convert_add_fusion.1, f32[96]{0:T(128)S(1)} %sqrt.38, f32[96]{0:T(128)S(1)} %get-tuple-element.50), kind=kLoop, calls=%fused_computation.19 | loop fusion | flops 3760128 | bytes 895104 | tf_op jit(solution)/shard_map/convert.7
  16.6 6.8 %multiply_convert_fusion.1 = (bf16[9,256,96]{1,2,0:T(8,128)(2,1)S(1)}, bf16[9,256,96]{1,2,0:T(8,128)(2,1)S(1)}) fusion(f32[96]{0:T(128)S(1)} %get-tuple-element.51, f32[9,256]{1,0:T(8,128)S(1)} %convert_add_fusion, f32[96]{0:T(128)S(1)} %sqrt.38, f32[96]{0:T(128)S(1)} %get-tuple-element.50), kind=kLoop, calls=%fused_computation.15 | loop fusion | flops 3760128 | bytes 895104 | tf_op jit(solution)/shard_map/convert.3
  23.5 0.7 fusion.19
  25.9 1.1 convolution_convert_fusion.1
  27.4 1.0 copy.61
  28.4 6.6 %all-to-all-start = ((bf16[2,3,16,1536]{3,0,1,2:T(2,128)(2,1)}), bf16[2,3,16,1536]{3,0,1,2:T(2,128)(2,1)S(1)}, u32[]{:S(2)}, u32[]{:S(2)}) async-start(bf16[2,3,16,1536]{3,0,1,2:T(2,128)(2,1)} %copy.61), calls=%async_computation | async-start | bytes 589824 | tf_op jit(solution)/shard_map/all_to_all | solution.py:120
  35.0 1.2 and_convert_fusion
  36.3 4.4 %all-to-all-done = bf16[2,3,16,1536]{3,0,1,2:T(2,128)(2,1)S(1)} async-done(((bf16[2,3,16,1536]{3,0,1,2:T(2,128)(2,1)}), bf16[2,3,16,1536]{3,0,1,2:T(2,128)(2,1)S(1)}, u32[]{:S(2)}, u32[]{:S(2)}) %all-to-all-start) | async-done | bytes 294944 | tf_op jit(solution)/shard_map/all_to_all | solution.py:120
  42.0 19.4 %copy.66 = bf16[3,1,24576]{0,1,2:T(2,128)(2,1)} copy(bf16[3,1,24576]{2,0,1:T(4,128)(2,1)S(1)} %convert_element_type.135) | data formatting | bytes 294912 | tf_op jit(solution)/shard_map/convert_element_type | solution.py:97
  61.9 134.9 %reduce.5 = bf16[24576,3]{1,0:T(8,128)(2,1)} reduce(bf16[24576,1,3]{2,1,0:T(2,128)(2,1)} %bitcast.152, bf16[]{:T(256)} %broadcast.341), dimensions={1}, to_apply=%bitcast.148.reduce_sub_computation | reduce | bytes 294914
  196.9 10.0 %reshape.529 = bf16[16,2,2304]{2,1,0:T(2,128)(2,1)} reshape(bf16[24576,3]{1,0:T(8,128)(2,1)} %reduce.5) | data formatting | bytes 294912
  206.9 5.5 %all-to-all-start.1 = ((bf16[16,2,2304]{2,1,0:T(2,128)(2,1)}), bf16[16,2,2304]{2,1,0:T(2,128)(2,1)S(1)}, u32[]{:S(2)}, u32[]{:S(2)}) async-start(bf16[16,2,2304]{2,1,0:T(2,128)(2,1)} %reshape.529), calls=%async_computation.1 | async-start | bytes 294912 | tf_op jit(solution)/shard_map/all_to_all | solution.py:125
  212.7 4.8 %all-to-all-done.1 = bf16[16,2,2304]{2,1,0:T(2,128)(2,1)S(1)} async-done(((bf16[16,2,2304]{2,1,0:T(2,128)(2,1)}), bf16[16,2,2304]{2,1,0:T(2,128)(2,1)S(1)}, u32[]{:S(2)}, u32[]{:S(2)}) %all-to-all-start.1) | async-done | bytes 147488 | tf_op jit(solution)/shard_map/all_to_all | solution.py:125
  217.5 14.4 %reshape.530 = bf16[24576,1,3]{2,1,0:T(2,128)(2,1)} reshape(bf16[16,2,2304]{2,1,0:T(2,128)(2,1)S(1)} %all-to-all-done.1) | data formatting | bytes 294912
  231.9 23.3 %copy.67 = bf16[3,1,24576]{2,0,1:T(4,128)(2,1)S(1)} copy(bf16[3,1,24576]{0,1,2:T(2,128)(2,1)} %bitcast.151) | data formatting | bytes 294912 | tf_op jit(solution)/shard_map/all_to_all | solution.py:125
  257.3 3.5 %collective-permute-start.2 = (bf16[3,16,1024]{2,1,0:T(8,128)(2,1)S(1)}, bf16[3,16,1024]{2,1,0:T(8,128)(2,1)S(1)}, u32[]{:S(2)}, u32[]{:S(2)}) collective-permute-start(bf16[3,16,1024]{2,1,0:T(8,128)(2,1)S(1)} %get-tuple-element.41), channel_id=1, source_target_pairs={{0,1},{1,2},{2,3},{3,4},{4,5},{5,6},{6,7},{7,8},{8,9},{9,10},{10,1... | collective-permute-start | bytes 294920 | tf_op jit(solution)/shard_map/ppermute | solution.py:31
  260.9 1.9 collective-permute-start.3
  262.8 5.5 %collective-permute-done.3 = bf16[3,16,1024]{2,1,0:T(8,128)(2,1)S(1)} collective-permute-done((bf16[3,16,1024]{2,1,0:T(8,128)(2,1)S(1)}, bf16[3,16,1024]{2,1,0:T(8,128)(2,1)S(1)}, u32[]{:S(2)}, u32[]{:S(2)}) %collective-permute-start.3) | collective-permute-done | bytes 98336 | tf_op jit(solution)/shard_map/ppermute | solution.py:31
  269.5 76.0 %all_to_all.23 = bf16[3,64,2048]{2,0,1:T(4,128)(2,1)S(1)} all-to-all(bf16[3,64,2048]{2,0,1:T(4,128)(2,1)S(1)} %copy.76), channel_id=1, replica_groups=mesh['space'=32,'tm'=16] {'space'}, dimensions={1} | all-to-all | bytes 1572864 | tf_op jit(solution)/shard_map/all_to_all | solution.py:150
  345.5 1.5 copy.77
  (52 shorter events, 7.5 us)
Async XLA Ops:
  0.0 23.4 %copy-start = (s32[16,2]{0,1:T(2,128)S(1)}, s32[16,2]{0,1:T(2,128)}, u32[]{:S(2)}) copy-start(s32[16,2]{0,1:T(2,128)} %param.10) | copy-start | bytes 388
  0.0 24.7 %copy-start.1 = (bf16[2,3,16,2048]{3,2,1,0:T(8,128)(2,1)S(1)}, bf16[2,3,16,2048]{3,2,1,0:T(8,128)(2,1)}, u32[]{:S(2)}) copy-start(bf16[2,3,16,2048]{3,2,1,0:T(8,128)(2,1)} %param.8) | copy-start | bytes 1179652
  1.1 23.6 %collective-permute-start = (bf16[2,3,16,1024]{3,2,1,0:T(8,128)(2,1)S(1)}, bf16[2,3,16,1024]{3,2,1,0:T(8,128)(2,1)S(1)}, u32[]{:S(2)}, u32[]{:S(2)}) collective-permute-start(bf16[2,3,16,1024]{3,2,1,0:T(8,128)(2,1)S(1)} %get-tuple-element.42), channel_id=1, source_target_pairs={{0,1},{1,2},{2,3},{3,4},{4,5},{5,6},{6,7},{7,8},{8,9},{9,10},{10,1... | collective-permute-start | bytes 589832 | tf_op jit(solution)/shard_map/ppermute | solution.py:20
  3.9 20.8 %collective-permute-start.1 = (bf16[2,3,16,1024]{3,2,1,0:T(8,128)(2,1)S(1)}, bf16[2,3,16,1024]{3,2,1,0:T(8,128)(2,1)S(1)}, u32[]{:S(2)}, u32[]{:S(2)}) collective-permute-start(bf16[2,3,16,1024]{3,2,1,0:T(8,128)(2,1)S(1)} %get-tuple-element.43), channel_id=1, source_target_pairs={{1,0},{2,1},{3,2},{4,3},{5,4},{6,5},{7,6},{8,7},{9,8},{10,9},{11,1... | collective-permute-start | bytes 589832 | tf_op jit(solution)/shard_map/ppermute | solution.py:23
  28.4 12.3 %all-to-all-start = ((bf16[2,3,16,1536]{3,0,1,2:T(2,128)(2,1)}), bf16[2,3,16,1536]{3,0,1,2:T(2,128)(2,1)S(1)}, u32[]{:S(2)}, u32[]{:S(2)}) async-start(bf16[2,3,16,1536]{3,0,1,2:T(2,128)(2,1)} %copy.61), calls=%async_computation | async-start | bytes 589824 | tf_op jit(solution)/shard_map/all_to_all | solution.py:120
  196.9 15.5 %copy-start.2 = (s32[16,1]{0,1:T(1,128)S(1)}, s32[16,1]{0,1:T(1,128)}, u32[]{:S(2)}) copy-start(s32[16,1]{0,1:T(1,128)} %param.9) | copy-start | bytes 196
  206.9 10.6 %all-to-all-start.1 = ((bf16[16,2,2304]{2,1,0:T(2,128)(2,1)}), bf16[16,2,2304]{2,1,0:T(2,128)(2,1)S(1)}, u32[]{:S(2)}, u32[]{:S(2)}) async-start(bf16[16,2,2304]{2,1,0:T(2,128)(2,1)} %reshape.529), calls=%async_computation.1 | async-start | bytes 294912 | tf_op jit(solution)/shard_map/all_to_all | solution.py:125
  257.3 5.5 %collective-permute-start.2 = (bf16[3,16,1024]{2,1,0:T(8,128)(2,1)S(1)}, bf16[3,16,1024]{2,1,0:T(8,128)(2,1)S(1)}, u32[]{:S(2)}, u32[]{:S(2)}) collective-permute-start(bf16[3,16,1024]{2,1,0:T(8,128)(2,1)S(1)} %get-tuple-element.41), channel_id=1, source_target_pairs={{0,1},{1,2},{2,3},{3,4},{4,5},{5,6},{6,7},{7,8},{8,9},{9,10},{10,1... | collective-permute-start | bytes 294920 | tf_op jit(solution)/shard_map/ppermute | solution.py:31
  260.9 7.5 %collective-permute-start.3 = (bf16[3,16,1024]{2,1,0:T(8,128)(2,1)S(1)}, bf16[3,16,1024]{2,1,0:T(8,128)(2,1)S(1)}, u32[]{:S(2)}, u32[]{:S(2)}) collective-permute-start(bf16[3,16,1024]{2,1,0:T(8,128)(2,1)S(1)} %get-tuple-element.40), channel_id=1, source_target_pairs={{1,0},{2,1},{3,2},{4,3},{5,4},{6,5},{7,6},{8,7},{9,8},{10,9},{11,1... | collective-permute-start | bytes 294920 | tf_op jit(solution)/shard_map/ppermute | solution.py:31
where the time goes:
time: 348 us; the launch traced here: 347 us
  other arithmetic  156 us (45%)
  blocking collectives  76 us (22%)
  local copies, waits for them, and re-layouts  75.2 us (22%)
  starting transfers between devices  22.8 us (7%)
  waiting for transfers between devices  14.8 us (4%)
    unnamed x1, other arithmetic  135 us
    all_to_all x1, blocking collectives, on_device(): lax.all_to_all(outgoing, 'space', split_axis=1, concat_axis=1, tiled=True)  76 us
    unnamed x18, local copies, waits for them, and re-layouts  26 us
    all_to_all x1, local copies, waits for them, and re-layouts, on_device(): lax.all_to_all(adjoint_local, 'tm', split_axis=2, concat_axis=1, tiled=True)  23.3 us
    convert_element_type x2, local copies, waits for them, and re-layouts, misfit(): joined.reshape(joined.shape[:2] + (joined.shape[2] * joined.shape[3],))  19.7 us
    another operation x4, other arithmetic  13.9 us
  transfers between devices with their start and end apart: 6, of which 3 were waited for; matrix products, arithmetic and copies ran while one was open for 6% of the time, Pallas kernels for 0%

commit v1 on v0

--- a/solution.py
+++ b/solution.py
@@ -100,6 +100,16 @@
 
 
 def on_device(recordings, owner, valid_range, bin_mask):
+
+    def manage_row(vec, peer_axis):
+        placed = jnp.concatenate(
+            lax.all_to_all(
+                jnp.stack(jnp.split(vec, lax.axis_size(peer_axis), axis=2), axis=0), peer_axis, 0, 0
+            ),
+            axis=1,
+        )
+        return placed
+
     table = cq_kernel(KERNEL, BINS)
     margin = HALO // HOP
     width = 2 * BINS
@@ -122,7 +132,7 @@
     frames_all = pieces.shape[3] // width
     local_coefs = pieces.astype(jnp.float32).reshape(2, items, rec_group, frames_all, width)
     adjoint_local = misfit(local_coefs, weight)
-    adjoint_back = lax.all_to_all(adjoint_local, "tm", split_axis=2, concat_axis=1, tiled=True)
+    adjoint_back = manage_row(adjoint_local, "tm")
     adjoint_frames = adjoint_back.reshape(comps, rec_dev, frames_dev, width)
     ext = synthesise(adjoint_frames, table, frames_dev)
     flat = ext.reshape(comps, rec_dev, (frames_dev + 2 * margin) * HOP)

time: 348 us -> 155 us (0.45)
  other arithmetic: 156 us -> 20.8 us
  local copies, waits for them, and re-layouts: 75.2 us -> 17.3 us
    unnamed x1 -> x0, other arithmetic: 135 us -> none
    all_to_all x1 -> x0, local copies, waits for them, and re-layouts: 23.3 us -> none  [on_device(): lax.all_to_all(adjoint_local, 'tm', split_axis=2, concat_axis=1, tiled=True)]
    convert_element_type x2 -> x1, local copies, waits for them, and re-layouts: 19.7 us -> 0.25 us  [misfit(): joined.reshape(joined.shape[:2] + (joined.shape[2] * joined.shape[3],))]
    unnamed x18 -> x30, local copies, waits for them, and re-layouts: 26 us -> 10.1 us
  transfers between devices with their start and end apart: 6 -> 6, of which waited for: 3 -> 3; matrix products, arithmetic and copies ran while one was open for 6% -> 13% of each run, Pallas kernels for 0% -> 0%
where the time goes in v1:
time: 155 us; the launch traced here: 154 us
  blocking collectives  76 us (49%)
  starting transfers between devices  22.8 us (15%)
  other arithmetic  20.8 us (13%)
  local copies, waits for them, and re-layouts  17.3 us (11%)
  waiting for transfers between devices  14.8 us (10%)
  matrix products  2.21 us (1%)
    all_to_all x1, blocking collectives, on_device(): lax.all_to_all(outgoing, 'space', split_axis=1, concat_axis=1, tiled=True)  76 us
    another operation x4, other arithmetic  13.9 us
    unnamed x30, local copies, waits for them, and re-layouts  10.1 us
    all_to_all x1, starting transfers between devices, on_device(): lax.all_to_all(packed, 'tm', split_axis=2, concat_axis=3, tiled=True)  6.61 us
    ppermute x2, waiting for transfers between devices, shifted(): return lax.ppermute(block, axis, route)  5.51 us
    all_to_all x1, starting transfers between devices, manage_row(): lax.all_to_all(jnp.stack(jnp.split(vec, lax.axis_size(peer_axis), axis=2)...  5.5 us
    ppermute x2, starting transfers between devices, shifted(): return lax.ppermute(block, axis, route)  5.46 us
    all_to_all x1, waiting for transfers between devices, manage_row(): lax.all_to_all(jnp.stack(jnp.split(vec, lax.axis_size(peer_axis), axis=2)...  4.97 us
  transfers between devices with their start and end apart: 6, of which 3 were waited for; matrix products, arithmetic and copies ran while one was open for 13% of the time, Pallas kernels for 0%

profile of v1, /device:TPU:25, one launch (start us, length us, event | category | flops | bytes accessed | tf_op | source)
XLA Modules:
  0.0 154.3 jit_solution(5021923016003726282)
XLA Ops:
  0.0 1.1 fusion.24
  1.1 2.8 %collective-permute-start = (bf16[2,3,16,1024]{3,2,1,0:T(8,128)(2,1)S(1)}, bf16[2,3,16,1024]{3,2,1,0:T(8,128)(2,1)S(1)}, u32[]{:S(2)}, u32[]{:S(2)}) collective-permute-start(bf16[2,3,16,1024]{3,2,1,0:T(8,128)(2,1)S(1)} %get-tuple-element.42), channel_id=1, source_target_pairs={{0,1},{1,2},{2,3},{3,4},{4,5},{5,6},{6,7},{7,8},{8,9},{9,10},{10,1... | collective-permute-start | bytes 589832 | tf_op jit(solution)/shard_map/ppermute | solution.py:20
  3.9 2.5 %collective-permute-start.1 = (bf16[2,3,16,1024]{3,2,1,0:T(8,128)(2,1)S(1)}, bf16[2,3,16,1024]{3,2,1,0:T(8,128)(2,1)S(1)}, u32[]{:S(2)}, u32[]{:S(2)}) collective-permute-start(bf16[2,3,16,1024]{3,2,1,0:T(8,128)(2,1)S(1)} %get-tuple-element.43), channel_id=1, source_target_pairs={{1,0},{2,1},{3,2},{4,3},{5,4},{6,5},{7,6},{8,7},{9,8},{10,9},{11,1... | collective-permute-start | bytes 589832 | tf_op jit(solution)/shard_map/ppermute | solution.py:23
  6.5 3.4 %multiply_reduce_fusion = f32[96]{0:T(128)S(1)} fusion(f32[96]{0:T(128)S(1)} %get-tuple-element.50, f32[2304]{0:T(1024)S(1)} %convert_add_fusion.1), kind=kLoop, calls=%fused_computation.20 | loop fusion | flops 1990560 | bytes 9984 | tf_op jit(solution)/shard_map/reduce_sum | solution.py:43
  9.9 6.7 %multiply_convert_fusion.3 = (bf16[2304,96]{0,1:T(8,128)(2,1)S(1)}, bf16[2304,96]{0,1:T(8,128)(2,1)S(1)}) fusion(f32[96]{0:T(128)S(1)} %get-tuple-element.51, f32[2304]{0:T(1024)S(1)} %convert_add_fusion.1, f32[96]{0:T(128)S(1)} %sqrt.38, f32[96]{0:T(128)S(1)} %get-tuple-element.50), kind=kLoop, calls=%fused_computation.19 | loop fusion | flops 3760128 | bytes 895104 | tf_op jit(solution)/shard_map/convert.7
  16.6 6.8 %multiply_convert_fusion.1 = (bf16[9,256,96]{1,2,0:T(8,128)(2,1)S(1)}, bf16[9,256,96]{1,2,0:T(8,128)(2,1)S(1)}) fusion(f32[96]{0:T(128)S(1)} %get-tuple-element.51, f32[9,256]{1,0:T(8,128)S(1)} %convert_add_fusion, f32[96]{0:T(128)S(1)} %sqrt.38, f32[96]{0:T(128)S(1)} %get-tuple-element.50), kind=kLoop, calls=%fused_computation.15 | loop fusion | flops 3760128 | bytes 895104 | tf_op jit(solution)/shard_map/convert.3
  23.5 0.7 fusion.19
  26.0 1.1 convolution_convert_fusion.1
  27.4 1.0 copy.75
  28.5 6.6 %all-to-all-start = ((bf16[2,3,16,1536]{3,0,1,2:T(2,128)(2,1)}), bf16[2,3,16,1536]{3,0,1,2:T(2,128)(2,1)S(1)}, u32[]{:S(2)}, u32[]{:S(2)}) async-start(bf16[2,3,16,1536]{3,0,1,2:T(2,128)(2,1)} %copy.75), calls=%async_computation | async-start | bytes 589824 | tf_op jit(solution)/shard_map/all_to_all | solution.py:130
  35.1 1.2 and_convert_fusion
  36.4 4.4 %all-to-all-done = bf16[2,3,16,1536]{3,0,1,2:T(2,128)(2,1)S(1)} async-done(((bf16[2,3,16,1536]{3,0,1,2:T(2,128)(2,1)}), bf16[2,3,16,1536]{3,0,1,2:T(2,128)(2,1)S(1)}, u32[]{:S(2)}, u32[]{:S(2)}) %all-to-all-start) | async-done | bytes 294944 | tf_op jit(solution)/shard_map/all_to_all | solution.py:130
  42.1 0.6 constant_dynamic-update-slice_fusion.15
  42.7 0.6 constant_dynamic-update-slice_fusion.14
  43.3 0.6 constant_dynamic-update-slice_fusion.13
  51.8 5.5 %all-to-all-start.1 = ((bf16[16,3,1,1536]{3,1,2,0:T(4,128)(2,1)}), bf16[16,3,1,1536]{3,1,2,0:T(4,128)(2,1)S(1)}, u32[]{:S(2)}, u32[]{:S(2)}) async-start(bf16[16,3,1,1536]{3,1,2,0:T(4,128)(2,1)} %constant_dynamic-update-slice_fusion), calls=%async_computation.1 | async-start | bytes 393216 | tf_op jit(solution)/shard_map/all_to_all | solution.py:106
  57.5 5.0 %all-to-all-done.1 = bf16[16,3,1,1536]{3,1,2,0:T(4,128)(2,1)S(1)} async-done(((bf16[16,3,1,1536]{3,1,2,0:T(4,128)(2,1)}), bf16[16,3,1,1536]{3,1,2,0:T(4,128)(2,1)S(1)}, u32[]{:S(2)}, u32[]{:S(2)}) %all-to-all-start.1) | async-done | bytes 147488 | tf_op jit(solution)/shard_map/all_to_all | solution.py:106
  62.7 0.6 fusion.5
  64.6 3.5 %collective-permute-start.2 = (bf16[3,16,1024]{2,1,0:T(8,128)(2,1)S(1)}, bf16[3,16,1024]{2,1,0:T(8,128)(2,1)S(1)}, u32[]{:S(2)}, u32[]{:S(2)}) collective-permute-start(bf16[3,16,1024]{2,1,0:T(8,128)(2,1)S(1)} %get-tuple-element.41), channel_id=1, source_target_pairs={{0,1},{1,2},{2,3},{3,4},{4,5},{5,6},{6,7},{7,8},{8,9},{9,10},{10,1... | collective-permute-start | bytes 294920 | tf_op jit(solution)/shard_map/ppermute | solution.py:31
  68.2 1.9 %collective-permute-start.3 = (bf16[3,16,1024]{2,1,0:T(8,128)(2,1)S(1)}, bf16[3,16,1024]{2,1,0:T(8,128)(2,1)S(1)}, u32[]{:S(2)}, u32[]{:S(2)}) collective-permute-start(bf16[3,16,1024]{2,1,0:T(8,128)(2,1)S(1)} %get-tuple-element.40), channel_id=1, source_target_pairs={{1,0},{2,1},{3,2},{4,3},{5,4},{6,5},{7,6},{8,7},{9,8},{10,9},{11,1... | collective-permute-start | bytes 294920 | tf_op jit(solution)/shard_map/ppermute | solution.py:31
  70.2 5.5 %collective-permute-done.3 = bf16[3,16,1024]{2,1,0:T(8,128)(2,1)S(1)} collective-permute-done((bf16[3,16,1024]{2,1,0:T(8,128)(2,1)S(1)}, bf16[3,16,1024]{2,1,0:T(8,128)(2,1)S(1)}, u32[]{:S(2)}, u32[]{:S(2)}) %collective-permute-start.3) | collective-permute-done | bytes 98336 | tf_op jit(solution)/shard_map/ppermute | solution.py:31
  76.2 0.7 copy.89
  76.9 76.0 %all_to_all.19 = bf16[3,64,2048]{2,0,1:T(4,128)(2,1)S(1)} all-to-all(bf16[3,64,2048]{2,0,1:T(4,128)(2,1)S(1)} %copy.89), channel_id=1, replica_groups=mesh['space'=32,'tm'=16] {'space'}, dimensions={1} | all-to-all | bytes 1572864 | tf_op jit(solution)/shard_map/all_to_all | solution.py:160
  152.9 1.5 copy.90
  (63 shorter events, 13.6 us)
Async XLA Ops:
  0.0 23.4 %copy-start = (s32[16,2]{0,1:T(2,128)S(1)}, s32[16,2]{0,1:T(2,128)}, u32[]{:S(2)}) copy-start(s32[16,2]{0,1:T(2,128)} %param.10) | copy-start | bytes 388
  0.0 24.8 %copy-start.1 = (bf16[2,3,16,2048]{3,2,1,0:T(8,128)(2,1)S(1)}, bf16[2,3,16,2048]{3,2,1,0:T(8,128)(2,1)}, u32[]{:S(2)}) copy-start(bf16[2,3,16,2048]{3,2,1,0:T(8,128)(2,1)} %param.8) | copy-start | bytes 1179652
  1.1 23.7 %collective-permute-start = (bf16[2,3,16,1024]{3,2,1,0:T(8,128)(2,1)S(1)}, bf16[2,3,16,1024]{3,2,1,0:T(8,128)(2,1)S(1)}, u32[]{:S(2)}, u32[]{:S(2)}) collective-permute-start(bf16[2,3,16,1024]{3,2,1,0:T(8,128)(2,1)S(1)} %get-tuple-element.42), channel_id=1, source_target_pairs={{0,1},{1,2},{2,3},{3,4},{4,5},{5,6},{6,7},{7,8},{8,9},{9,10},{10,1... | collective-permute-start | bytes 589832 | tf_op jit(solution)/shard_map/ppermute | solution.py:20
  3.9 20.9 %collective-permute-start.1 = (bf16[2,3,16,1024]{3,2,1,0:T(8,128)(2,1)S(1)}, bf16[2,3,16,1024]{3,2,1,0:T(8,128)(2,1)S(1)}, u32[]{:S(2)}, u32[]{:S(2)}) collective-permute-start(bf16[2,3,16,1024]{3,2,1,0:T(8,128)(2,1)S(1)} %get-tuple-element.43), channel_id=1, source_target_pairs={{1,0},{2,1},{3,2},{4,3},{5,4},{6,5},{7,6},{8,7},{9,8},{10,9},{11,1... | collective-permute-start | bytes 589832 | tf_op jit(solution)/shard_map/ppermute | solution.py:23
  27.1 30.1 %copy-start.2 = (s32[16,1]{0,1:T(1,128)S(1)}, s32[16,1]{0,1:T(1,128)}, u32[]{:S(2)}) copy-start(s32[16,1]{0,1:T(1,128)} %param.9) | copy-start | bytes 196
  28.5 12.3 %all-to-all-start = ((bf16[2,3,16,1536]{3,0,1,2:T(2,128)(2,1)}), bf16[2,3,16,1536]{3,0,1,2:T(2,128)(2,1)S(1)}, u32[]{:S(2)}, u32[]{:S(2)}) async-start(bf16[2,3,16,1536]{3,0,1,2:T(2,128)(2,1)} %copy.75), calls=%async_computation | async-start | bytes 589824 | tf_op jit(solution)/shard_map/all_to_all | solution.py:130
  51.8 10.8 %all-to-all-start.1 = ((bf16[16,3,1,1536]{3,1,2,0:T(4,128)(2,1)}), bf16[16,3,1,1536]{3,1,2,0:T(4,128)(2,1)S(1)}, u32[]{:S(2)}, u32[]{:S(2)}) async-start(bf16[16,3,1,1536]{3,1,2,0:T(4,128)(2,1)} %constant_dynamic-update-slice_fusion), calls=%async_computation.1 | async-start | bytes 393216 | tf_op jit(solution)/shard_map/all_to_all | solution.py:106
  64.6 5.5 %collective-permute-start.2 = (bf16[3,16,1024]{2,1,0:T(8,128)(2,1)S(1)}, bf16[3,16,1024]{2,1,0:T(8,128)(2,1)S(1)}, u32[]{:S(2)}, u32[]{:S(2)}) collective-permute-start(bf16[3,16,1024]{2,1,0:T(8,128)(2,1)S(1)} %get-tuple-element.41), channel_id=1, source_target_pairs={{0,1},{1,2},{2,3},{3,4},{4,5},{5,6},{6,7},{7,8},{8,9},{9,10},{10,1... | collective-permute-start | bytes 294920 | tf_op jit(solution)/shard_map/ppermute | solution.py:31
  68.2 7.5 %collective-permute-start.3 = (bf16[3,16,1024]{2,1,0:T(8,128)(2,1)S(1)}, bf16[3,16,1024]{2,1,0:T(8,128)(2,1)S(1)}, u32[]{:S(2)}, u32[]{:S(2)}) collective-permute-start(bf16[3,16,1024]{2,1,0:T(8,128)(2,1)S(1)} %get-tuple-element.40), channel_id=1, source_target_pairs={{1,0},{2,1},{3,2},{4,3},{5,4},{6,5},{7,6},{8,7},{9,8},{10,9},{11,1... | collective-permute-start | bytes 294920 | tf_op jit(solution)/shard_map/ppermute | solution.py:31
